TPU v7x, 32 devices: a whole 2x2x4 slice. The times are simulated.
32 devices in a mesh: grp: 2 (over core), blk: 16 (over z, y, x).
Axes of the slice: x: 2, y: 2, z: 4, core: 2. Of those that a mesh axis runs over, the one named last changes fastest.
Arguments:
- queries: bfloat16 [256, 4096], P('blk'), may hold values from -30 to 30
- turn_pos: int32 [256], P('blk'), may hold values from 32768 to 33280, as said below
- cached_key_rows: bfloat16 [65536, 1024], P(('grp', 'blk')), may hold values from -21 to 21
- cached_value_rows: bfloat16 [65536, 1024], P(('grp', 'blk')), may hold values from -6 to 6
- turn_keys: bfloat16 [256, 1024], P(('grp', 'blk')), may hold values from -33 to 33
- turn_values: bfloat16 [256, 1024], P(('grp', 'blk')), may hold values from -6 to 6
- cache_pos: int32 [65536], P(('grp', 'blk')), may hold values from 0 to 65535, each once
Outputs:
- attended: bfloat16 [256, 4096], P('blk')
Inputs may be any that keep to these rules, and one draw needn't show every extreme that they name: turn_pos rises strictly by one or two from each token to the next.
All inputs are finite; a program needn't handle non-finite values.
Results may differ from a plain program's by a relative error of at most 0.0026.
Values may be sent and summed in bfloat16 or wider, within the bound.
A program may use at most 128 MiB of HBM per device.

v0:
```python
import math

import jax
import jax.numpy as jnp
from jax import lax
from jax.sharding import PartitionSpec as P

QUERY_HEADS = 32
KEY_VALUE_HEADS = 8
HEAD_SIZE = 128


NEGATIVE_FLOOR = -1e30


def on_device(
    queries, turn_pos, cached_key_rows, cached_value_rows, turn_keys, turn_values, cache_pos
):
    query_group = QUERY_HEADS // KEY_VALUE_HEADS
    scale = 1.0 / math.sqrt(HEAD_SIZE)
    every_query, all_pos = (
        lax.all_gather(queries, "blk", axis=0, tiled=True),
        lax.all_gather(turn_pos, "blk", axis=0, tiled=True),
    )
    turn_index = every_query.shape[0]
    query_head_rows = every_query.reshape(turn_index, KEY_VALUE_HEADS, query_group, HEAD_SIZE)
    slots = cached_key_rows.shape[0]
    block_width = min(slots, 512)
    block_count = slots // block_width
    key_block_list = cached_key_rows.reshape(block_count, block_width, KEY_VALUE_HEADS, HEAD_SIZE)
    value_block_list = cached_value_rows.reshape(
        block_count, block_width, KEY_VALUE_HEADS, HEAD_SIZE
    )
    pos_blocks = cache_pos.reshape(block_count, block_width)
    fresh_rows = turn_keys.shape[0]
    fresh_keys = turn_keys.reshape(fresh_rows, KEY_VALUE_HEADS, HEAD_SIZE)
    fresh_values = turn_values.reshape(fresh_rows, KEY_VALUE_HEADS, HEAD_SIZE)
    first = lax.axis_index(("grp", "blk")) * fresh_rows
    visible_turn_mask = (first + jnp.arange(fresh_rows, dtype=jnp.int32))[None, :] <= jnp.arange(
        turn_index, dtype=jnp.int32
    )[:, None]

    def masked_scores(keys, visible):
        scores = (
            jnp.einsum("tkgd,ckd->tkgc", query_head_rows, keys, preferred_element_type=jnp.float32)
            * scale
        )
        return jnp.where(visible[:, None, None, :], scores, NEGATIVE_FLOOR)

    def peak_step(current, items):
        keys, slot_pos = items
        visible = slot_pos[None, :] < all_pos[:, None]
        return (jnp.maximum(current, jnp.max(masked_scores(keys, visible), -1)), None)

    start_peak = jnp.max(masked_scores(fresh_keys, visible_turn_mask), -1)
    local_top, unused = lax.scan(peak_step, start_peak, (key_block_list, pos_blocks))
    highest = lax.pmax(local_top, ("grp", "blk"))

    def update(loop_carry, keys, values, visible):
        total, accum = loop_carry
        scores = (
            jnp.einsum("tkgd,ckd->tkgc", query_head_rows, keys, preferred_element_type=jnp.float32)
            * scale
        )
        weight = jnp.where(visible[:, None, None, :], jnp.exp(scores - highest[..., None]), 0.0)
        total = total + jnp.sum(weight, -1)
        accum = accum + jnp.einsum(
            "tkgc,ckd->tkgd",
            weight.astype(jnp.bfloat16),
            values,
            preferred_element_type=jnp.float32,
        )
        return (total, accum)

    def block_step(loop_carry, items):
        keys, values, slot_pos = items
        visible = slot_pos[None, :] < all_pos[:, None]
        return (update(loop_carry, keys, values, visible), None)

    start_carry = (
        jnp.zeros((turn_index, KEY_VALUE_HEADS, query_group), jnp.float32),
        jnp.zeros((turn_index, KEY_VALUE_HEADS, query_group, HEAD_SIZE), jnp.float32),
    )
    loop_carry, unused = lax.scan(
        block_step, start_carry, (key_block_list, value_block_list, pos_blocks)
    )
    total, accum = update(loop_carry, fresh_keys, fresh_values, visible_turn_mask)
    rows_out = turn_index // lax.axis_size("blk")
    row_start = lax.axis_index("blk") * rows_out
    flat_accum = accum.reshape(turn_index, QUERY_HEADS * HEAD_SIZE)
    flat_total = total.reshape(turn_index, QUERY_HEADS)
    sum_accum, sum_total = lax.psum((flat_accum, flat_total), ("grp", "blk"))
    mine_total = lax.dynamic_slice_in_dim(sum_total, row_start, rows_out, 0)
    mine_accum = lax.dynamic_slice_in_dim(sum_accum, row_start, rows_out, 0)
    result = mine_accum.reshape(rows_out, QUERY_HEADS, HEAD_SIZE) / mine_total[..., None]
    return result.reshape(rows_out, QUERY_HEADS * HEAD_SIZE).astype(jnp.bfloat16)


def solution(mesh):
    placed = (
        P("blk", None),
        P("blk"),
        P(("grp", "blk"), None),
        P(("grp", "blk"), None),
        P(("grp", "blk"), None),
        P(("grp", "blk"), None),
        P(("grp", "blk")),
    )
    return jax.shard_map(
        on_device, mesh=mesh, in_specs=placed, out_specs=P("blk", None), check_vma=False
    )
```

profile of v0, /device:TPU:0, one launch (start us, length us, event | category | flops | bytes accessed | tf_op | source)
XLA Modules:
  0.0 403.7 jit_solution(12653480880768015736)
XLA Ops:
  8.0 3.3 copy.39
  11.3 2.9 copy.26
  14.2 5.3 %copy.40 = bf16[256,8,8,128]{3,2,1,0:T(8,128)(2,1)} copy(bf16[256,8,8,128]{3,1,2,0:T(8,128)(2,1)} %bitcast.108) | data formatting | bytes 8388608
  21.0 16.2 %all-reduce = s32[256]{0:T(256)S(1)} all-reduce(s32[256]{0:T(256)S(1)} %dynamic-update-slice), channel_id=1, replica_groups=mesh['grp'=2,'blk'=16] {'blk'}, use_global_device_ids=true, to_apply=%add | all-reduce | flops 256 | bytes 2048
  37.2 36.4 %all-gather.2.cloned.1.call-done = bf16[256,4096]{1,0:T(8,128)(2,1)} async-done(((bf16[16,4096]{1,0:T(8,128)(2,1)}), bf16[256,4096]{1,0:T(8,128)(2,1)}) %all-gather.2.cloned.1.call-update) | async-done | bytes 2097168 | tf_op jit(solution)/shard_map/all_gather | solution.py:22
  73.6 3.3 copy.22
  76.9 2.4 copy.27
  79.3 1.1 select_reduce_fusion
  80.4 18.1 %while.23 = (s32[]{:T(128)}, f32[256,8,4]{0,2,1:T(4,128)S(1)}, s32[4,512]{1,0:T(4,128)S(1)}, s32[256]{0:T(256)S(1)}, bf16[4,512,8,128]{3,1,2,0:T(8,128)(2,1)}, /*index=5*/bf16[256,8,4,128]{3,0,2,1:T(8,128)(2,1)}, s32[]{:T(128)}) while((s32[]{:T(128)}, f32[256,8,4]{0,2,1:T(4,128)S(1)}, s32[4,512]{1,0:T(4,128)S(1)}, s32[256]{0:T(256)S(1)}, ...), condition=%wide.region_3.4_spmd, body=%wide.region_1.3_spmd.sunk | while | flops 1086455808 | bytes 3546205 | solution.py:56
  80.6 4.3 %fusion.46 = f32[256,8,4]{0,2,1:T(4,128)S(1)} fusion(bf16[256,8,4,128]{3,0,2,1:T(8,128)(2,1)} %get-tuple-element.297, pred[256,512]{0,1:T(8,128)(4,1)S(1)} %broadcast_compare_fusion.4, bf16[4,512,8,128]{3,1,2,0:T(8,128)(2,1)} %get-tuple-element.296, s32[]{:T(128)S(6)} %copy.48), kind=kOutput, calls=%fused_computation.1.clone.1 | convolution fusion | flops 1086316544 | bytes 3309572 | tf_op jit(solution)/shard_map/while/body/eval_jaxpr/tkgd,ckd->tkgc/dot_general | solution.py:45
  85.1 4.3 %fusion.46 = f32[256,8,4]{0,2,1:T(4,128)S(1)} fusion(bf16[256,8,4,128]{3,0,2,1:T(8,128)(2,1)} %get-tuple-element.297, pred[256,512]{0,1:T(8,128)(4,1)S(1)} %broadcast_compare_fusion.4, bf16[4,512,8,128]{3,1,2,0:T(8,128)(2,1)} %get-tuple-element.296, s32[]{:T(128)S(6)} %copy.48), kind=kOutput, calls=%fused_computation.1.clone.1 | convolution fusion | flops 1086316544 | bytes 3309572 | tf_op jit(solution)/shard_map/while/body/eval_jaxpr/tkgd,ckd->tkgc/dot_general | solution.py:45
  89.6 4.3 %fusion.46 = f32[256,8,4]{0,2,1:T(4,128)S(1)} fusion(bf16[256,8,4,128]{3,0,2,1:T(8,128)(2,1)} %get-tuple-element.297, pred[256,512]{0,1:T(8,128)(4,1)S(1)} %broadcast_compare_fusion.4, bf16[4,512,8,128]{3,1,2,0:T(8,128)(2,1)} %get-tuple-element.296, s32[]{:T(128)S(6)} %copy.48), kind=kOutput, calls=%fused_computation.1.clone.1 | convolution fusion | flops 1086316544 | bytes 3309572 | tf_op jit(solution)/shard_map/while/body/eval_jaxpr/tkgd,ckd->tkgc/dot_general | solution.py:45
  94.2 4.3 %fusion.46 = f32[256,8,4]{0,2,1:T(4,128)S(1)} fusion(bf16[256,8,4,128]{3,0,2,1:T(8,128)(2,1)} %get-tuple-element.297, pred[256,512]{0,1:T(8,128)(4,1)S(1)} %broadcast_compare_fusion.4, bf16[4,512,8,128]{3,1,2,0:T(8,128)(2,1)} %get-tuple-element.296, s32[]{:T(128)S(6)} %copy.48), kind=kOutput, calls=%fused_computation.1.clone.1 | convolution fusion | flops 1086316544 | bytes 3309572 | tf_op jit(solution)/shard_map/while/body/eval_jaxpr/tkgd,ckd->tkgc/dot_general | solution.py:45
  98.5 39.6 %pmax.7 = f32[256,8,4]{0,2,1:T(4,128)S(1)} all-reduce(f32[256,8,4]{0,2,1:T(4,128)S(1)} %get-tuple-element.85), channel_id=1, replica_groups=mesh['grp'=2,'blk'=16] {'grp','blk'}, use_global_device_ids=true, to_apply=%region_4.5 | all-reduce | flops 8192 | bytes 65536 | tf_op jit(solution)/shard_map/pmax | solution.py:57
  138.1 104.1 %while.24 = (s32[]{:T(128)}, f32[256,8,4]{0,2,1:T(4,128)S(1)}, f32[256,8,4,128]{0,3,2,1:T(8,128)}, s32[4,512]{1,0:T(4,128)S(1)}, s32[256]{0:T(256)S(1)}, /*index...) while((s32[]{:T(128)}, f32[256,8,4]{0,2,1:T(4,128)S(1)}, ...), condition=%wide.region_7.8_spmd.clone, body=%wide.region_5.7_spmd.clone.sunk | while | flops 2183274496 | bytes 50928776 | solution.py:84
  138.3 11.6 %fusion.50 = (f32[256,8,4]{0,2,1:T(4,128)S(1)}, f32[8,512,256,4]{2,1,3,0:T(8,128)}) fusion(f32[256,8,4]{0,2,1:T(4,128)S(1)} %get-tuple-element.328, pred[256,512]{0,1:T(8,128)(4,1)S(1)} %broadcast_compare_fusion.5, bf16[256,8,4,128]{3,0,2,1:T(8,128)(2,1)} %get-tuple-element.327, bf16[4,512,8,128]{3,1,2,0:T(8,128)(2,1)} %get-tuple-element.326, ...), kind=kOutput, calls=%fused_computation.11.clone.1 | convolution fusion | flops 1090510848 | bytes 20119556 | tf_op jit(solution)/shard_map/while/body/eval_jaxpr/tkgd,ckd->tkgc/dot_general | solution.py:62
  149.9 1.3 constant_dynamic-slice_fusion.9
  151.9 11.4 %bitcast_add_fusion.3 = f32[256,8,4,128]{0,3,2,1:T(8,128)} fusion(f32[256,8,4,128]{0,3,2,1:T(8,128)} %get-tuple-element.312, f32[8,512,256,4]{2,1,3,0:T(8,128)} %get-tuple-element.277, f32[256,8,4]{0,2,1:T(4,128)S(1)} %get-tuple-element.328, pred[256,512]{0,1:T(8,128)(4,1)S(1)} %broadcast_compare_fusion.5, pred[]{:T(512)S(6)} %compare.3, ...), kind=kOutput, calls=%fused_computation.17.clone.1 | convolution fusion | flops 1092616192 | bytes 26378240 | tf_op jit(solution)/shard_map/while/body/eval_jaxpr/tkgc,ckd->tkgd/dot_general | solution.py:67
  163.4 11.6 %fusion.50 = (f32[256,8,4]{0,2,1:T(4,128)S(1)}, f32[8,512,256,4]{2,1,3,0:T(8,128)}) fusion(f32[256,8,4]{0,2,1:T(4,128)S(1)} %get-tuple-element.328, pred[256,512]{0,1:T(8,128)(4,1)S(1)} %broadcast_compare_fusion.5, bf16[256,8,4,128]{3,0,2,1:T(8,128)(2,1)} %get-tuple-element.327, bf16[4,512,8,128]{3,1,2,0:T(8,128)(2,1)} %get-tuple-element.326, ...), kind=kOutput, calls=%fused_computation.11.clone.1 | convolution fusion | flops 1090510848 | bytes 20119556 | tf_op jit(solution)/shard_map/while/body/eval_jaxpr/tkgd,ckd->tkgc/dot_general | solution.py:62
  175.0 1.3 constant_dynamic-slice_fusion.9
  177.0 12.6 %bitcast_add_fusion.3 = f32[256,8,4,128]{0,3,2,1:T(8,128)} fusion(f32[256,8,4,128]{0,3,2,1:T(8,128)} %get-tuple-element.312, f32[8,512,256,4]{2,1,3,0:T(8,128)} %get-tuple-element.277, f32[256,8,4]{0,2,1:T(4,128)S(1)} %get-tuple-element.328, pred[256,512]{0,1:T(8,128)(4,1)S(1)} %broadcast_compare_fusion.5, pred[]{:T(512)S(6)} %compare.3, ...), kind=kOutput, calls=%fused_computation.17.clone.1 | convolution fusion | flops 1092616192 | bytes 26378240 | tf_op jit(solution)/shard_map/while/body/eval_jaxpr/tkgc,ckd->tkgd/dot_general | solution.py:67
  189.7 11.6 %fusion.50 = (f32[256,8,4]{0,2,1:T(4,128)S(1)}, f32[8,512,256,4]{2,1,3,0:T(8,128)}) fusion(f32[256,8,4]{0,2,1:T(4,128)S(1)} %get-tuple-element.328, pred[256,512]{0,1:T(8,128)(4,1)S(1)} %broadcast_compare_fusion.5, bf16[256,8,4,128]{3,0,2,1:T(8,128)(2,1)} %get-tuple-element.327, bf16[4,512,8,128]{3,1,2,0:T(8,128)(2,1)} %get-tuple-element.326, ...), kind=kOutput, calls=%fused_computation.11.clone.1 | convolution fusion | flops 1090510848 | bytes 20119556 | tf_op jit(solution)/shard_map/while/body/eval_jaxpr/tkgd,ckd->tkgc/dot_general | solution.py:62
  201.3 1.3 constant_dynamic-slice_fusion.9
  203.3 12.6 %bitcast_add_fusion.3 = f32[256,8,4,128]{0,3,2,1:T(8,128)} fusion(f32[256,8,4,128]{0,3,2,1:T(8,128)} %get-tuple-element.312, f32[8,512,256,4]{2,1,3,0:T(8,128)} %get-tuple-element.277, f32[256,8,4]{0,2,1:T(4,128)S(1)} %get-tuple-element.328, pred[256,512]{0,1:T(8,128)(4,1)S(1)} %broadcast_compare_fusion.5, pred[]{:T(512)S(6)} %compare.3, ...), kind=kOutput, calls=%fused_computation.17.clone.1 | convolution fusion | flops 1092616192 | bytes 26378240 | tf_op jit(solution)/shard_map/while/body/eval_jaxpr/tkgc,ckd->tkgd/dot_general | solution.py:67
  216.0 11.6 %fusion.50 = (f32[256,8,4]{0,2,1:T(4,128)S(1)}, f32[8,512,256,4]{2,1,3,0:T(8,128)}) fusion(f32[256,8,4]{0,2,1:T(4,128)S(1)} %get-tuple-element.328, pred[256,512]{0,1:T(8,128)(4,1)S(1)} %broadcast_compare_fusion.5, bf16[256,8,4,128]{3,0,2,1:T(8,128)(2,1)} %get-tuple-element.327, bf16[4,512,8,128]{3,1,2,0:T(8,128)(2,1)} %get-tuple-element.326, ...), kind=kOutput, calls=%fused_computation.11.clone.1 | convolution fusion | flops 1090510848 | bytes 20119556 | tf_op jit(solution)/shard_map/while/body/eval_jaxpr/tkgd,ckd->tkgc/dot_general | solution.py:62
  227.6 1.3 constant_dynamic-slice_fusion.9
  229.6 12.6 %bitcast_add_fusion.3 = f32[256,8,4,128]{0,3,2,1:T(8,128)} fusion(f32[256,8,4,128]{0,3,2,1:T(8,128)} %get-tuple-element.312, f32[8,512,256,4]{2,1,3,0:T(8,128)} %get-tuple-element.277, f32[256,8,4]{0,2,1:T(4,128)S(1)} %get-tuple-element.328, pred[256,512]{0,1:T(8,128)(4,1)S(1)} %broadcast_compare_fusion.5, pred[]{:T(512)S(6)} %compare.3, ...), kind=kOutput, calls=%fused_computation.17.clone.1 | convolution fusion | flops 1092616192 | bytes 26378240 | tf_op jit(solution)/shard_map/while/body/eval_jaxpr/tkgc,ckd->tkgd/dot_general | solution.py:67
  242.2 4.9 %bitcast_add_fusion.1 = f32[256,8,4,128]{0,3,2,1:T(8,128)} fusion(f32[256,8,4,128]{0,3,2,1:T(8,128)} %get-tuple-element.86, f32[256,8,4,8]{0,3,2,1:T(8,128)S(1)} %copy-done.1, f32[256,8,4]{0,2,1:T(4,128)S(1)} %get-tuple-element.339, pred[256,8]{0,1:T(8,128)(4,1)S(1)} %copy-done.3, bf16[8,1024]{1,0:T(8,128)(2,1)S(1)} %copy-done), kind=kOutput, calls=%fused_computation.29 | convolution fusion | flops 18022400 | bytes 8701952 | tf_op jit(solution)/shard_map/tkgc,ckd->tkgd/dot_general | solution.py:67
  247.1 5.6 %copy.29 = f32[256,4096]{1,0:T(8,128)} copy(f32[256,4096]{0,1:T(8,128)} %bitcast.105) | data formatting | bytes 8388608 | tf_op jit(solution)/shard_map/reshape | solution.py:90
  252.9 40.5 %psum.15 = f32[256,32]{0,1:T(8,128)S(1)} all-reduce(f32[256,32]{0,1:T(8,128)S(1)} %reshape.106), channel_id=1, replica_groups=mesh['grp'=2,'blk'=16] {'grp','blk'}, use_global_device_ids=true, to_apply=%region_10.11 | all-reduce | flops 8192 | bytes 65536 | tf_op jit(solution)/shard_map/psum | solution.py:92
  293.6 101.4 %all-reduce.3.cloned.1.call-done = f32[256,4096]{1,0:T(8,128)} async-done(((f32[256,4096]{1,0:T(8,128)}), f32[256,4096]{1,0:T(8,128)}) %all-reduce.3.cloned.1.call-update) | async-done | bytes 4194320 | tf_op jit(solution)/shard_map/psum | solution.py:92
  395.1 1.8 fusion.24
  (60 shorter events, 6.9 us)
Async XLA Ops:
  6.5 235.7 %copy-start = (bf16[8,1024]{1,0:T(8,128)(2,1)S(1)}, bf16[8,1024]{1,0:T(8,128)(2,1)}, u32[]{:S(2)}) copy-start(bf16[8,1024]{1,0:T(8,128)(2,1)} %param.16) | copy-start | bytes 49156
  6.5 67.1 %all-gather.2.cloned.1.call-start = ((), (), s32[]{:S(2)}) async-start(), calls=%async_computation | async-start | bytes 2228224 | tf_op jit(solution)/shard_map/all_gather | solution.py:22
  7.3 387.7 %all-reduce.3.cloned.1.call-start = ((), (), s32[]{:S(2)}) async-start(), calls=%async_computation.1 | async-start | bytes 8388608 | tf_op jit(solution)/shard_map/psum | solution.py:92
  14.2 5.3 %copy-start.6 = (u32[32]{0:T(128)S(1)}, u32[32]{0:T(128)}, u32[]{:S(2)}) copy-start(u32[32]{0:T(128)} %constant.58) | copy-start | bytes 388
  14.2 6.5 %copy-start.5 = (s32[16]{0:T(128)S(1)}, s32[16]{0:T(128)}, u32[]{:S(2)}) copy-start(s32[16]{0:T(128)} %param.12) | copy-start | bytes 196
  37.2 42.1 %copy-start.2 = (pred[256,8]{0,1:T(8,128)(4,1)}, pred[256,8]{0,1:T(8,128)(4,1)S(1)}, u32[]{:S(2)}) copy-start(pred[256,8]{0,1:T(8,128)(4,1)S(1)} %iota_compare_fusion) | copy-start | bytes 6148
  37.2 42.1 %copy-start.4 = (bf16[8,1024]{1,0:T(8,128)(2,1)S(1)}, bf16[8,1024]{1,0:T(8,128)(2,1)}, u32[]{:S(2)}) copy-start(bf16[8,1024]{1,0:T(8,128)(2,1)} %param.15) | copy-start | bytes 49156
  138.1 104.1 %copy-start.1 = (f32[256,8,4,8]{0,3,2,1:T(8,128)S(1)}, f32[256,8,4,8]{0,3,2,1:T(8,128)}, u32[]{:S(2)}) copy-start(f32[256,8,4,8]{0,3,2,1:T(8,128)} %get-tuple-element.181) | copy-start | bytes 786436
  138.1 104.1 %copy-start.3 = (pred[256,8]{0,1:T(8,128)(4,1)S(1)}, pred[256,8]{0,1:T(8,128)(4,1)}, u32[]{:S(2)}) copy-start(pred[256,8]{0,1:T(8,128)(4,1)} %copy-done.2) | copy-start | bytes 6148
Sparse Core Ops, SparseCore 0:
  10.1 63.4 all-gather.1
  252.9 142.0 all-reduce.2
where the time goes:
time: 405 us; the launch traced here: 404 us
  waiting for transfers between devices  139 us (34%)
  matrix products  119 us (29%)
  blocking collectives  96.2 us (24%)
  local copies, waits for them, and re-layouts  32.6 us (8%)
  between operations  14.2 us (4%)
    psum x1, waiting for transfers between devices, on_device(): sum_accum, sum_total = lax.psum((flat_accum, flat_total), ('grp', 'blk'))  101 us
    dot_general x5, matrix products, update(): jnp.einsum('tkgc,ckd->tkgd', weight.astype(jnp.bfloat16), values, preferr...  54 us
    dot_general x4, matrix products, update(): jnp.einsum('tkgd,ckd->tkgc', query_head_rows, keys, preferred_element_typ...  46.3 us
    psum x1, blocking collectives, on_device(): sum_accum, sum_total = lax.psum((flat_accum, flat_total), ('grp', 'blk'))  40.5 us
    pmax x1, blocking collectives, on_device(): highest = lax.pmax(local_top, ('grp', 'blk'))  39.6 us
    all_gather x1, waiting for transfers between devices, on_device(): lax.all_gather(queries, 'blk', axis=0, tiled=True)  36.4 us
    dot_general x5, matrix products, masked_scores(): jnp.einsum('tkgd,ckd->tkgc', query_head_rows, keys, preferred_element_typ...  18.4 us
    unnamed x1, blocking collectives  16.2 us
  transfers between devices with their start and end apart: 2, of which 2 were waited for; matrix products, arithmetic and copies ran while one was open for 3% of the time, Pallas kernels for 0%

commit v1 on v0

v1 whole, which is shorter than its diff:
```python
import functools
import math

import jax
import jax.numpy as jnp
from jax import lax
from jax.experimental import pallas as pl
from jax.experimental.pallas import tpu as pltpu
from jax.sharding import PartitionSpec as P

QUERY_HEADS = 32
KEY_VALUE_HEADS = 8
HEAD_SIZE = 128
GROUP = QUERY_HEADS // KEY_VALUE_HEADS
LANE = 128
BLOCK = 256
TURN_SPAN = 512
FAR = 1e9
LOW = -1e30
LOG2E = math.log2(math.e)
NT = (((1,), (1,)), ((), ()))


def _dot(a, b):
    return jnp.dot(a, b, preferred_element_type=jnp.float32)


def _dot_nt(a, b):
    return lax.dot_general(a, b, NT, preferred_element_type=jnp.float32)


def _rank(flags, slots):
    rows = slots // LANE
    upper = (
        lax.broadcasted_iota(jnp.int32, (LANE, LANE), 0)
        < lax.broadcasted_iota(jnp.int32, (LANE, LANE), 1)
    ).astype(jnp.bfloat16)
    inside = _dot(flags.astype(jnp.bfloat16), upper)
    counts = jnp.sum(flags, axis=1, keepdims=True)
    before = (
        lax.broadcasted_iota(jnp.int32, (rows, rows), 1)
        < lax.broadcasted_iota(jnp.int32, (rows, rows), 0)
    ).astype(jnp.bfloat16)
    ahead = _dot(before, jnp.broadcast_to(counts, (rows, LANE)).astype(jnp.bfloat16))
    return inside + ahead, jnp.sum(flags)


def _compact_kernel(
    base, slots, fresh, pos_ref, k_ref, v_ref, tk_ref, tv_ref, kc_ref, vc_ref, code_ref, count_ref
):
    pos = pos_ref[...] - base
    always = (pos < 0).astype(jnp.float32)
    maybe = ((pos >= 0) & (pos < TURN_SPAN)).astype(jnp.float32)
    rank_a, count_a = _rank(always, slots)
    rank_m, count_m = _rank(maybe, slots)
    count_a = count_a.astype(jnp.int32)
    count_m = count_m.astype(jnp.int32)
    count_ref[0] = count_a
    count_ref[1] = count_m
    dest_a = jnp.where(always > 0, rank_a.astype(jnp.int32), -1)
    dest_m = jnp.where(maybe > 0, rank_m.astype(jnp.int32) + count_a, -1)
    row_total = jnp.sum(always, axis=1, keepdims=True)
    del row_total
    kc_ref[pl.ds(0, LANE), :] = jnp.zeros((LANE, kc_ref.shape[1]), kc_ref.dtype)
    vc_ref[pl.ds(0, LANE), :] = jnp.zeros((LANE, vc_ref.shape[1]), vc_ref.dtype)
    window = BLOCK + LANE
    lanes = BLOCK // LANE
    for b in range(slots // BLOCK):
        start = jnp.sum(always[: b * lanes]).astype(jnp.int32) if b else jnp.int32(0)
        off = pl.multiple_of((start // LANE) * LANE, LANE)
        rows = lax.broadcasted_iota(jnp.int32, (window, LANE), 0) + off
        pick = jnp.concatenate(
            [
                (dest_a[b * lanes + i : b * lanes + i + 1, :] == rows)
                for i in range(lanes)
            ],
            axis=1,
        ).astype(jnp.float32).astype(jnp.bfloat16)
        for src, dst in ((k_ref, kc_ref), (v_ref, vc_ref)):
            got = _dot(pick, src[pl.ds(b * BLOCK, BLOCK), :]).astype(jnp.bfloat16)
            dst[pl.ds(off, LANE), :] = dst[pl.ds(off, LANE), :] + got[:LANE]
            dst[pl.ds(off + LANE, BLOCK), :] = got[LANE:]
    first = (count_a // LANE) * LANE
    for dst in (kc_ref, vc_ref):
        tail = pl.multiple_of(first + LANE, LANE)
        dst[pl.ds(tail, BLOCK), :] = jnp.zeros((BLOCK, dst.shape[1]), dst.dtype)
    total = count_a + count_m + fresh
    code = jnp.where(maybe > 0, pos + 1, 0)
    high, low = code // 32, code % 32

    def step(i, carry):
        off = pl.multiple_of(first + i * LANE, LANE)
        rows = lax.broadcasted_iota(jnp.int32, (LANE, LANE), 0) + off
        pick = jnp.concatenate(
            [(dest_m[j : j + 1, :] == rows) for j in range(slots // LANE)], axis=1
        ).astype(jnp.float32).astype(jnp.bfloat16)
        which = lax.broadcasted_iota(jnp.int32, (LANE, LANE), 1)
        turn_pick = (
            (which + (count_a + count_m) == rows) & (which < fresh)
        ).astype(jnp.float32).astype(jnp.bfloat16)
        keep = jnp.where(i == 0, 1.0, 0.0).astype(jnp.bfloat16)
        for src, turn, dst in ((k_ref, tk_ref, kc_ref), (v_ref, tv_ref, vc_ref)):
            got = (_dot(pick, src[...]) + _dot(turn_pick, turn[...])).astype(jnp.bfloat16)
            dst[pl.ds(off, LANE), :] = dst[pl.ds(off, LANE), :] * keep + got
            dst[pl.ds(off + LANE, BLOCK), :] = jnp.zeros((BLOCK, dst.shape[1]), dst.dtype)
        flat = jnp.concatenate([high[j : j + 1, :] for j in range(slots // LANE)], axis=1)
        flat_low = jnp.concatenate([low[j : j + 1, :] for j in range(slots // LANE)], axis=1)
        width = flat.shape[1]
        digits = jnp.concatenate(
            [jnp.broadcast_to(flat * 1.0, (8, width)), jnp.broadcast_to(flat_low * 1.0, (8, width))],
            axis=0,
        ).astype(jnp.bfloat16)
        got = _dot_nt(digits, pick)
        value = got[:8] * 32.0 + got[8:]
        place = lax.broadcasted_iota(jnp.int32, (8, LANE), 1) + off
        value = jnp.where(place < count_a, 0.0, jnp.where(place < count_a + count_m, value, FAR))
        code_ref[0:8, pl.ds(off, LANE)] = value
        turn_value = jnp.where(
            (place >= count_a + count_m) & (place < total),
            (place - (count_a + count_m)).astype(jnp.float32),
            FAR,
        )
        code_ref[8:16, pl.ds(off, LANE)] = turn_value
        return carry

    code_ref[...] = jnp.full(code_ref.shape, FAR, jnp.float32)
    lax.fori_loop(0, (total - first + LANE - 1) // LANE, step, 0)


def _attend_kernel(
    fresh, count_ref, q_ref, kc_ref, vc_ref, code_ref, lim_ref, out_ref, lse_ref, s_ref, m_ref, l_ref
):
    tokens = q_ref.shape[0]
    rows = GROUP * tokens
    heads = KEY_VALUE_HEADS
    factor = LOG2E / math.sqrt(HEAD_SIZE)
    count_a = count_ref[0]
    total = count_a + count_ref[1] + fresh
    plain = count_a // LANE
    chunks = (total + LANE - 1) // LANE

    lse_ref[...] = jnp.zeros_like(lse_ref)

    for k in range(heads):
        cols = slice(k * HEAD_SIZE, (k + 1) * HEAD_SIZE)
        m_ref[...] = jnp.full(m_ref.shape, LOW, jnp.float32)
        l_ref[...] = jnp.zeros_like(l_ref)

        def scores(i, masked):
            off = pl.multiple_of(i * LANE, LANE)
            key = kc_ref[pl.ds(off, LANE), cols]
            if masked:
                a = code_ref[0:1, pl.ds(off, LANE)]
                b = code_ref[8:9, pl.ds(off, LANE)]
                seen = (a < lim_ref[:, 0:1]) | (b < lim_ref[:, 1:2])
            for g in range(GROUP):
                h = k * GROUP + g
                s = _dot_nt(q_ref[:, h * HEAD_SIZE : (h + 1) * HEAD_SIZE], key)
                if masked:
                    s = jnp.where(seen, s, LOW)
                here = slice(g * tokens, (g + 1) * tokens)
                s_ref[i, here, :] = s
                m_ref[here, :] = jnp.maximum(m_ref[here, :], s)

        def open_body(i, c):
            scores(i, False)
            return c

        def masked_body(i, c):
            scores(i, True)
            return c

        lax.fori_loop(0, plain, open_body, 0)
        lax.fori_loop(plain, chunks, masked_body, 0)
        top = jnp.max(m_ref[...], axis=1, keepdims=True)
        m_ref[...] = jnp.broadcast_to(jnp.maximum(top, 0.1 * LOW), m_ref.shape)
        for g in range(GROUP):
            h = k * GROUP + g
            out_ref[:, h * HEAD_SIZE : (h + 1) * HEAD_SIZE] = jnp.zeros((tokens, HEAD_SIZE), jnp.float32)

        def weigh(i, c):
            off = pl.multiple_of(i * LANE, LANE)
            value = vc_ref[pl.ds(off, LANE), cols]
            for g in range(GROUP):
                h = k * GROUP + g
                here = slice(g * tokens, (g + 1) * tokens)
                w = jnp.exp2((s_ref[i, here, :] - m_ref[here, :]) * factor)
                l_ref[here, :] += w
                out_ref[:, h * HEAD_SIZE : (h + 1) * HEAD_SIZE] += _dot(w.astype(jnp.bfloat16), value)
            return c

        lax.fori_loop(0, chunks, weigh, 0)
        for g in range(GROUP):
            h = k * GROUP + g
            here = slice(g * tokens, (g + 1) * tokens)
            den = jnp.sum(l_ref[here, :], axis=1, keepdims=True)
            lane = lax.broadcasted_iota(jnp.int32, (tokens, LANE), 1)
            lse_ref[:, 0:LANE] = jnp.where(lane == h, m_ref[here, :] * factor, lse_ref[:, 0:LANE])
            lse_ref[:, LANE:] = jnp.where(lane == h, den, lse_ref[:, LANE:])


def on_device(
    queries, turn_pos, cached_key_rows, cached_value_rows, turn_keys, turn_values, cache_pos
):
    blk = lax.axis_size("blk")
    grp = lax.axis_size("grp")
    slots = cached_key_rows.shape[0]
    width = cached_key_rows.shape[1]
    fresh = turn_keys.shape[0]
    base = slots * grp * blk // 2
    size = -(-(slots + fresh) // LANE) * LANE + 2 * BLOCK
    every_query = lax.all_gather(queries, "blk", axis=0, tiled=True)
    all_pos = lax.all_gather(turn_pos, "blk", axis=0, tiled=True)
    tokens = every_query.shape[0]
    pad = ((0, LANE - fresh), (0, 0))
    vmem = pl.BlockSpec(memory_space=pltpu.VMEM)
    smem = pl.BlockSpec(memory_space=pltpu.SMEM)
    kc, vc, code, count = pl.pallas_call(
        functools.partial(_compact_kernel, base, slots, fresh),
        out_shape=(
            jax.ShapeDtypeStruct((size, width), jnp.bfloat16),
            jax.ShapeDtypeStruct((size, width), jnp.bfloat16),
            jax.ShapeDtypeStruct((16, size), jnp.float32),
            jax.ShapeDtypeStruct((2,), jnp.int32),
        ),
        in_specs=[vmem] * 5,
        out_specs=(vmem, vmem, vmem, smem),
        compiler_params=pltpu.CompilerParams(vmem_limit_bytes=40 * 2**20),
        name="compact",
    )(
        cache_pos.reshape(slots // LANE, LANE),
        cached_key_rows,
        cached_value_rows,
        jnp.pad(turn_keys, pad),
        jnp.pad(turn_values, pad),
    )
    rank = lax.axis_index(("grp", "blk"))
    limit = (all_pos - base + 1).astype(jnp.float32)
    index_limit = (jnp.arange(tokens, dtype=jnp.int32) - rank * fresh + 1).astype(jnp.float32)
    limits = jnp.stack([limit, index_limit], axis=1)
    rows = GROUP * tokens
    accum, stats = pl.pallas_call(
        functools.partial(_attend_kernel, fresh),
        out_shape=(
            jax.ShapeDtypeStruct((tokens, QUERY_HEADS * HEAD_SIZE), jnp.float32),
            jax.ShapeDtypeStruct((tokens, 2 * LANE), jnp.float32),
        ),
        in_specs=[smem] + [vmem] * 5,
        out_specs=(vmem, vmem),
        scratch_shapes=[
            pltpu.VMEM((size // LANE, rows, LANE), jnp.float32),
            pltpu.VMEM((rows, LANE), jnp.float32),
            pltpu.VMEM((rows, LANE), jnp.float32),
        ],
        compiler_params=pltpu.CompilerParams(vmem_limit_bytes=56 * 2**20),
        name="attend",
    )(count, every_query, kc, vc, code, limits)
    top, den = stats[:, :QUERY_HEADS], stats[:, LANE : LANE + QUERY_HEADS]
    highest = lax.pmax(top, ("grp", "blk"))
    alpha = jnp.exp2(top - highest)
    scaled = accum.reshape(tokens, QUERY_HEADS, HEAD_SIZE) * alpha[..., None]
    flat = scaled.reshape(tokens, QUERY_HEADS * HEAD_SIZE)
    both = jnp.concatenate([flat, den * alpha, jnp.zeros((tokens, LANE - QUERY_HEADS))], axis=1)
    mine = lax.psum_scatter(both, "blk", scatter_dimension=0, tiled=True)
    mine = lax.psum(mine, "grp")
    rows_out = mine.shape[0]
    num = mine[:, : QUERY_HEADS * HEAD_SIZE].reshape(rows_out, QUERY_HEADS, HEAD_SIZE)
    dens = mine[:, QUERY_HEADS * HEAD_SIZE : QUERY_HEADS * HEAD_SIZE + QUERY_HEADS]
    result = num / dens[..., None]
    return result.reshape(rows_out, QUERY_HEADS * HEAD_SIZE).astype(jnp.bfloat16)


def solution(mesh):
    placed = (
        P("blk", None),
        P("blk"),
        P(("grp", "blk"), None),
        P(("grp", "blk"), None),
        P(("grp", "blk"), None),
        P(("grp", "blk"), None),
        P(("grp", "blk")),
    )
    return jax.shard_map(
        on_device, mesh=mesh, in_specs=placed, out_specs=P("blk", None), check_vma=False
    )
```

time: 405 us -> 340 us (0.84)
  matrix products: 119 us -> 0 us
  Pallas kernels: 0 us -> 52.7 us
  waiting for transfers between devices: 139 us -> 185 us
  blocking collectives: 96.2 us -> 56.6 us
  local copies, waits for them, and re-layouts: 32.6 us -> 21.6 us
  other arithmetic: 3.29 us -> 8.92 us
    reduce_scatter x0 -> x1, waiting for transfers between devices: none -> 137 us  [on_device(): mine = lax.psum_scatter(both, 'blk', scatter_dimension=0, tiled=True)]
    dot_general x14 -> x0, matrix products: 119 us -> none  [the longest x5 54 us: update(): jnp.einsum('tkgc,ckd->tkgd', weight.astype(jnp.bfloat16), values, preferr...]
    psum x1, waiting for transfers between devices: 101 us -> 19.9 us  [on_device(): mine = lax.psum(mine, 'grp')]
    pallas_call x0 -> x2, Pallas kernels: none -> 52.7 us  [the longest x1 44.4 us: on_device(): pl.pallas_call(functools.partial(_attend_kernel, fresh), out_shape=(jax.S...]
    psum x1 -> x0, blocking collectives: 40.5 us -> none  [on_device(): sum_accum, sum_total = lax.psum((flat_accum, flat_total), ('grp', 'blk'))]
    all_gather x1, waiting for transfers between devices: 36.4 us -> 27.8 us  [on_device(): every_query = lax.all_gather(queries, 'blk', axis=0, tiled=True)]
    dynamic_slice x18 -> x0, local copies, waits for them, and re-layouts: 8.11 us -> none  [the longest x16 7.96 us: on_device(): lax.scan(peak_step, start_peak, (key_block_list, pos_blocks))]
    mul x0 -> x2, other arithmetic: none -> 7.12 us  [the longest x1 5.97 us: on_device(): scaled = accum.reshape(tokens, QUERY_HEADS, HEAD_SIZE) * alpha[..., None]]
  transfers between devices with their start and end apart: 2 -> 3, of which waited for: 2 -> 3; matrix products, arithmetic and copies ran while one was open for 3% -> 1% of each run, Pallas kernels for 0% -> 2%
where the time goes in v1:
time: 340 us; the launch traced here: 339 us
  waiting for transfers between devices  185 us (54%)
  blocking collectives  56.6 us (17%)
  Pallas kernels  52.7 us (16%)
  local copies, waits for them, and re-layouts  21.6 us (6%)
  between operations  13.9 us (4%)
  other arithmetic  8.92 us (3%)
    reduce_scatter x1, waiting for transfers between devices, on_device(): mine = lax.psum_scatter(both, 'blk', scatter_dimension=0, tiled=True)  137 us
    pallas_call x1, Pallas kernels, on_device(): pl.pallas_call(functools.partial(_attend_kernel, fresh), out_shape=(jax.S...  44.4 us
    pmax x1, blocking collectives, on_device(): highest = lax.pmax(top, ('grp', 'blk'))  40.4 us
    all_gather x1, waiting for transfers between devices, on_device(): every_query = lax.all_gather(queries, 'blk', axis=0, tiled=True)  27.8 us
    psum x1, waiting for transfers between devices, on_device(): mine = lax.psum(mine, 'grp')  19.9 us
    unnamed x1, blocking collectives  16.2 us
    unnamed x17, local copies, waits for them, and re-layouts  10.9 us
    pallas_call x1, Pallas kernels, on_device(): pl.pallas_call(functools.partial(_compact_kernel, base, slots, fresh), ou...  8.37 us
  transfers between devices with their start and end apart: 3, of which 3 were waited for; matrix products, arithmetic and copies ran while one was open for 1% of the time, Pallas kernels for 2%

profile of v1, /device:TPU:0, one launch (start us, length us, event | category | flops | bytes accessed | tf_op | source)
XLA Modules:
  0.0 339.2 jit_solution(1335720993154554919)
XLA Ops:
  6.5 0.7 all-gather.2.cloned.1.call-update
  7.3 0.0 reduce-scatter.2.cloned.1.call-start
  7.3 1.2 dynamic-slice
  9.2 0.9 dynamic-update-slice
  10.1 16.2 %all-reduce.2 = s32[256]{0:T(256)S(1)} all-reduce(s32[256]{0:T(256)S(1)} %dynamic-update-slice), channel_id=1, replica_groups=mesh['grp'=2,'blk'=16] {'blk'}, use_global_device_ids=true, to_apply=%add.2 | all-reduce | flops 256 | bytes 2048
  26.3 0.8 copy.9.lim_ref
  27.1 0.7 pad.7.tk_ref
  27.8 0.7 pad.8.tv_ref
  28.6 2.2 copy-done.1
  30.8 2.2 copy-done.2
  33.0 0.7 copy-done.4
  33.7 8.4 %compact.1 = (bf16[2688,1024]{1,0:T(8,128)(2,1)S(1)}, bf16[2688,1024]{1,0:T(8,128)(2,1)}, f32[16,2688]{1,0:T(8,128)S(1)}, s32[2]{0:T(128)S(1)}) custom-call(s32[16,128]{1,0:T(8,128)S(1)} %bitcast.11, bf16[2048,1024]{1,0:T(8,128)(2,1)S(1)} %copy-done.1, bf16[2048,1024]{1,0:T(8,128)(2,1)S(1)} %copy-done.2, bf16[128,1024]{1,0:T(8,128)(2,1)S(1)} %pad.7.tk_ref, ...), custom_call_target="tpu_custom_call" | custom-call | tf_op jit(solution)/shard_map/compact/pallas_call | solution.py:218
  42.0 2.5 copy-done
  44.5 0.7 copy-done.3
  45.2 0.5 copy-done.5
  45.7 27.8 %all-gather.2.cloned.1.call-done.q_ref = bf16[256,4096]{1,0:T(8,128)(2,1)} async-done(((bf16[16,4096]{1,0:T(8,128)(2,1)}), bf16[256,4096]{1,0:T(8,128)(2,1)}) %all-gather.2.cloned.1.call-update) | async-done | bytes 2097168 | tf_op jit(solution)/shard_map/all_gather | solution.py:212
  73.5 44.4 %attend.1 = (f32[256,4096]{1,0:T(8,128)}, f32[256,256]{1,0:T(8,128)}) custom-call(s32[2]{0:T(128)} %copy-done.5, bf16[256,4096]{1,0:T(8,128)(2,1)} %all-gather.2.cloned.1.call-done.q_ref, bf16[2688,1024]{1,0:T(8,128)(2,1)} %copy-done, bf16[2688,1024]{1,0:T(8,128)(2,1)} %get-tuple-element.13.vc_ref, f32[16,2688]{1,0:T(8,128)} %copy-done.3, f32[256,2]{1,0:T(8,128)} %copy.9.lim_ref), custom_call_target="tpu_custom_call" | custom-call | tf_op jit(solution)/shard_map/attend/pallas_call | solution.py:242
  117.9 0.9 slice.12
  118.8 40.4 %pmax.7 = f32[256,32]{1,0:T(8,128)S(1)} all-reduce(f32[256,32]{1,0:T(8,128)S(1)} %slice.12), channel_id=1, replica_groups=mesh['grp'=2,'blk'=16] {'grp','blk'}, use_global_device_ids=true, to_apply=%region_0.1 | all-reduce | flops 8192 | bytes 65536 | tf_op jit(solution)/shard_map/pmax | solution.py:259
  159.2 1.2 slice_multiply_fusion
  160.4 1.1 mul.22
  161.5 0.0 copy-done.6
  161.5 6.0 %bitcast_multiply_fusion = f32[256,4096]{1,0:T(8,128)} fusion(f32[256,4096]{1,0:T(8,128)S(1)} %copy-done.6, f32[32,8,32,128]{3,2,1,0:T(8,128)S(1)} %bitcast.12), kind=kLoop, calls=%fused_computation | loop fusion | flops 1048576 | bytes 12582912 | tf_op jit(solution)/shard_map/mul | solution.py:261
  167.5 5.6 %concatenate.3 = f32[256,4224]{1,0:T(8,128)} concatenate(f32[256,4096]{1,0:T(8,128)} %bitcast_multiply_fusion, f32[256,32]{1,0:T(8,128)S(1)} %get-tuple-element.17, f32[256,96]{1,0:T(8,128)S(1)} %broadcast_in_dim.2), dimensions={1} | concatenate | bytes 8650752 | tf_op jit(solution)/shard_map/concatenate | solution.py:263
  173.1 0.0 reduce-scatter.2.cloned.1.call-update
  173.1 0.0 all-reduce.5.cloned.1.call-start
  173.2 137.0 %reduce-scatter.2.cloned.1.call-done = f32[16,4224]{1,0:T(8,128)} async-done(((f32[256,4224]{1,0:T(8,128)}), f32[16,4224]{1,0:T(8,128)}) %reduce-scatter.2.cloned.1.call-update) | async-done | bytes 270352 | tf_op jit(solution)/shard_map/reduce_scatter | solution.py:264
  310.1 0.0 all-reduce.5.cloned.1.call-update
  310.1 19.9 %all-reduce.5.cloned.1.call-done = f32[16,4224]{1,0:T(8,128)} async-done(((f32[16,4224]{1,0:T(8,128)}), f32[16,4224]{1,0:T(8,128)}) %all-reduce.5.cloned.1.call-update) | async-done | bytes 270352 | tf_op jit(solution)/shard_map/psum | solution.py:265
  330.1 0.7 slice.17
  330.8 0.1 div.11
  330.9 1.8 fusion
  (13 shorter events, 0.0 us)
Async XLA Ops:
  6.5 67.0 %all-gather.2.cloned.1.call-start = ((), (), s32[]{:S(2)}) async-start(), calls=%async_computation.1 | async-start | bytes 2228224 | tf_op jit(solution)/shard_map/all_gather | solution.py:212
  7.3 302.9 %reduce-scatter.2.cloned.1.call-start = ((), (), s32[]{:S(2)}) async-start(), calls=%async_computation.2 | async-start | bytes 4595712 | tf_op jit(solution)/shard_map/reduce_scatter | solution.py:264
  28.6 2.2 copy-start.1
  30.8 2.2 copy-start.2
  33.0 0.7 copy-start.4
  42.0 2.5 copy-start
  44.5 0.7 copy-start.3
  45.2 0.5 copy-start.5
  159.2 2.3 copy-start.6
  173.1 156.9 %all-reduce.5.cloned.1.call-start = ((), (), s32[]{:S(2)}) async-start(), calls=%async_computation.3 | async-start | bytes 540672 | tf_op jit(solution)/shard_map/psum | solution.py:265
Sparse Core Ops, SparseCore 0:
  10.1 63.3 all-gather.1
  173.2 136.8 reduce-scatter.1
  312.6 17.4 all-reduce.4

commit v2 on v1

--- a/solution.py
+++ b/solution.py
@@ -17,6 +17,8 @@
 TURN_SPAN = 512
 FAR = 1e9
 LOW = -1e30
+TINY = 1e-30
+MESH = pl.DeviceIdType.MESH
 LOG2E = math.log2(math.e)
 NT = (((1,), (1,)), ((), ()))
 
@@ -59,8 +61,6 @@
     count_ref[1] = count_m
     dest_a = jnp.where(always > 0, rank_a.astype(jnp.int32), -1)
     dest_m = jnp.where(maybe > 0, rank_m.astype(jnp.int32) + count_a, -1)
-    row_total = jnp.sum(always, axis=1, keepdims=True)
-    del row_total
     kc_ref[pl.ds(0, LANE), :] = jnp.zeros((LANE, kc_ref.shape[1]), kc_ref.dtype)
     vc_ref[pl.ds(0, LANE), :] = jnp.zeros((LANE, vc_ref.shape[1]), vc_ref.dtype)
     window = BLOCK + LANE
@@ -128,7 +128,7 @@
 
 
 def _attend_kernel(
-    fresh, count_ref, q_ref, kc_ref, vc_ref, code_ref, lim_ref, out_ref, lse_ref, s_ref, m_ref, l_ref
+    fresh, count_ref, first_ref, q_ref, kc_ref, vc_ref, code_ref, lim_ref, out_ref, lse_ref, s_ref, m_ref, l_ref
 ):
     tokens = q_ref.shape[0]
     rows = GROUP * tokens
@@ -140,6 +140,8 @@
     chunks = (total + LANE - 1) // LANE
 
     lse_ref[...] = jnp.zeros_like(lse_ref)
+    token = lax.broadcasted_iota(jnp.int32, (tokens, LANE), 0)
+    turn_limit = (token - first_ref[0] + 1).astype(jnp.float32)
 
     for k in range(heads):
         cols = slice(k * HEAD_SIZE, (k + 1) * HEAD_SIZE)
@@ -152,7 +154,7 @@
             if masked:
                 a = code_ref[0:1, pl.ds(off, LANE)]
                 b = code_ref[8:9, pl.ds(off, LANE)]
-                seen = (a < lim_ref[:, 0:1]) | (b < lim_ref[:, 1:2])
+                seen = (a < lim_ref[...]) | (b < turn_limit)
             for g in range(GROUP):
                 h = k * GROUP + g
                 s = _dot_nt(q_ref[:, h * HEAD_SIZE : (h + 1) * HEAD_SIZE], key)
@@ -195,8 +197,273 @@
             here = slice(g * tokens, (g + 1) * tokens)
             den = jnp.sum(l_ref[here, :], axis=1, keepdims=True)
             lane = lax.broadcasted_iota(jnp.int32, (tokens, LANE), 1)
-            lse_ref[:, 0:LANE] = jnp.where(lane == h, m_ref[here, :] * factor, lse_ref[:, 0:LANE])
-            lse_ref[:, LANE:] = jnp.where(lane == h, den, lse_ref[:, LANE:])
+            both = jnp.where(lane == QUERY_HEADS + h, den, lse_ref[...])
+            lse_ref[...] = jnp.where(lane == h, m_ref[here, :] * factor, both)
+            hcols = slice(h * HEAD_SIZE, (h + 1) * HEAD_SIZE)
+            out_ref[:, hcols] = out_ref[:, hcols] * (1.0 / jnp.maximum(den, TINY))
+
+
+def _orders(grp_index, bits):
+    odd = grp_index % 2
+    if bits < 2:
+        return [jnp.int32(2**b) for b in range(bits)]
+    return [1 + odd, 2 - odd] + [jnp.int32(2**b) for b in range(2, bits)]
+
+
+def _greet(me, grp_index, grp, worths):
+    barrier = pltpu.get_barrier_semaphore()
+    for w in worths:
+        side = (me // w) % 2
+        pl.semaphore_signal(
+            barrier, inc=1, device_id=(grp_index, me + (1 - 2 * side) * w), device_id_type=MESH
+        )
+    for d in range(1, grp):
+        pl.semaphore_signal(
+            barrier, inc=1, device_id=((grp_index + d) % grp, me), device_id_type=MESH
+        )
+    pl.semaphore_wait(barrier, len(worths) + grp - 1)
+
+
+def _gather_kernel(
+    blk, grp, q_ref, p_ref, out_ref, pos_ref, local_sem, send_sem, recv_sem, psend, precv, csend, crecv
+):
+    me, mine = lax.axis_index("blk"), lax.axis_index("grp")
+    bits = blk.bit_length() - 1
+    worths = _orders(mine, bits)[::-1]
+    width = q_ref.shape[1] // grp
+    own = pltpu.make_async_copy(q_ref, out_ref.at[me], local_sem)
+    own.start()
+    pos_ref[me] = p_ref[...]
+    _greet(me, mine, grp, worths)
+    own.wait()
+    cols = pl.ds(pl.multiple_of(mine * width, LANE), width)
+
+    def core_copies(index, slot):
+        made = []
+        for d in range(1, grp):
+            made.append(
+                pltpu.make_async_remote_copy(
+                    src_ref=out_ref.at[index, :, cols],
+                    dst_ref=out_ref.at[index, :, cols],
+                    send_sem=csend.at[slot * (grp - 1) + d - 1],
+                    recv_sem=crecv.at[slot * (grp - 1) + d - 1],
+                    device_id=((mine + d) % grp, me),
+                    device_id_type=MESH,
+                )
+            )
+        return made
+
+    started, cores = [], []
+    held = [(me, None)]
+    slot = 0
+    for w in worths:
+        side = (me // w) % 2
+        step = (1 - 2 * side) * w
+        coming = []
+        for index, arrival in held:
+            if arrival is not None and not arrival[2][0]:
+                _land(arrival, index, core_copies, cores)
+            pair = []
+            for ref, sends, recvs in (
+                (out_ref.at[index, :, cols], send_sem, recv_sem),
+                (pos_ref.at[index], psend, precv),
+            ):
+                pair.append(
+                    pltpu.make_async_remote_copy(
+                        src_ref=ref,
+                        dst_ref=ref,
+                        send_sem=sends.at[slot],
+                        recv_sem=recvs.at[slot],
+                        device_id=(mine, me + step),
+                        device_id_type=MESH,
+                    )
+                )
+            for c in pair:
+                c.start()
+            started += pair
+            coming.append((index + step, (pair, slot, [False])))
+            slot += 1
+        held = held + coming
+    for index, arrival in held:
+        if arrival is not None and not arrival[2][0]:
+            _land(arrival, index, core_copies, cores)
+    for c in started:
+        c.wait_send()
+    for c in cores:
+        c.wait()
+
+
+def _land(arrival, index, core_copies, cores):
+    pair, slot, done = arrival
+    for c in pair:
+        c.wait_recv()
+    more = core_copies(index, slot)
+    for c in more:
+        c.start()
+    cores.extend(more)
+    done[0] = True
+
+
+def _merge_stats(a, b):
+    lane = lax.broadcasted_iota(jnp.int32, a.shape, 1)
+    top = jnp.maximum(a, b)
+    wa = pltpu.roll(a, LANE - QUERY_HEADS, 1) * jnp.exp2(a - top)
+    wb = pltpu.roll(b, LANE - QUERY_HEADS, 1) * jnp.exp2(b - top)
+    wa = jnp.where(lane < QUERY_HEADS, wa, 0.0)
+    wb = jnp.where(lane < QUERY_HEADS, wb, 0.0)
+    den = wa + wb
+    inverse = 1.0 / jnp.maximum(den, TINY)
+    merged = jnp.where(lane < QUERY_HEADS, top, pltpu.roll(den, QUERY_HEADS, 1))
+    return wa * inverse, wb * inverse, merged
+
+
+def _reduce_kernel(
+    blk, grp, acc_in, st_in, out_ref, acc, st, stage, stage_st, land, land_st, final, sends, recvs, ssends, srecvs, fsend, frecv
+):
+    me, mine = lax.axis_index("blk"), lax.axis_index("grp")
+    bits, gbits = blk.bit_length() - 1, grp.bit_length() - 1
+    worths = _orders(mine, bits)
+    rows, total = acc_in.shape[1], acc_in.shape[2]
+    _greet(me, mine, grp, worths)
+    width = total
+    origin = 0
+    number = 0
+    wire = stage.dtype
+    source, source_st = acc_in, st_in
+    at = 0
+    at_st = 0
+    waits = []
+
+    def send(size_cols, first, count, device):
+        nonlocal number
+        made = (
+            pltpu.make_async_remote_copy(
+                src_ref=stage.at[pl.ds(first, count)],
+                dst_ref=land.at[pl.ds(first, count)],
+                send_sem=sends.at[number],
+                recv_sem=recvs.at[number],
+                device_id=device,
+                device_id_type=MESH,
+            ),
+            pltpu.make_async_remote_copy(
+                src_ref=stage_st.at[pl.ds(at_st, count // (size_cols // unit))],
+                dst_ref=land_st.at[pl.ds(at_st, count // (size_cols // unit))],
+                send_sem=ssends.at[number],
+                recv_sem=srecvs.at[number],
+                device_id=device,
+                device_id_type=MESH,
+            ),
+        )
+        number += 1
+        for c in made:
+            c.start()
+        waits.extend(made)
+        return made
+
+    unit = total // grp
+    for b in range(gbits):
+        half = width // 2
+        side = (mine // 2**b) % 2
+        partner = mine + (1 - 2 * side) * 2**b
+        keep = pl.multiple_of(origin + side * half, LANE)
+        give = pl.multiple_of(origin + (1 - side) * half, LANE)
+        parts = half // unit
+        base, base_st = at, at_st
+
+        def pack(i, c):
+            for p in range(parts):
+                stage[base + i * parts + p] = source[i, :, pl.ds(pl.multiple_of(give + p * unit, LANE), unit)].astype(wire)
+            stage_st[base_st + i] = source_st[i]
+            return c
+
+        lax.fori_loop(0, blk, pack, 0)
+        made = send(half, at, blk * parts, (partner, me))
+        for c in made:
+            c.wait_recv()
+        heads = half // HEAD_SIZE
+        first_head = keep // HEAD_SIZE
+
+        def merge(i, c):
+            ca, cb, both = _merge_stats(source_st[i], land_st[base_st + i])
+            shift = (LANE - first_head) % LANE
+            ca, cb = pltpu.roll(ca, shift, 1), pltpu.roll(cb, shift, 1)
+            for h in range(heads):
+                p, o = divmod(h * HEAD_SIZE, unit)
+                acc[i, :, pl.ds(pl.multiple_of(keep + h * HEAD_SIZE, LANE), HEAD_SIZE)] = (
+                    ca[:, h : h + 1] * source[i, :, pl.ds(pl.multiple_of(keep + h * HEAD_SIZE, LANE), HEAD_SIZE)]
+                    + cb[:, h : h + 1] * land[base + i * parts + p, :, o : o + HEAD_SIZE].astype(jnp.float32)
+                )
+            st[i] = both
+            return c
+
+        lax.fori_loop(0, blk, merge, 0)
+        source, source_st = acc, st
+        origin = keep
+        width = half
+        at += blk * parts
+        at_st += blk
+    cols = pl.ds(pl.multiple_of(origin, LANE), unit)
+    first_head = origin // HEAD_SIZE
+    shift = (LANE - first_head) % LANE
+    heads = unit // HEAD_SIZE
+    count = blk
+    for s, w in enumerate(worths):
+        side = (me // w) % 2
+        partner = me + (1 - 2 * side) * w
+        place = (w if s == 0 else 1)
+        half = count // 2
+        base, base_st = at, at_st
+
+        def pick(i, which):
+            return (i // place) * (2 * place) + which * place + i % place
+
+        def pack(i, c):
+            j = pick(i, 1 - side)
+            stage[base + i] = acc[j, :, cols].astype(wire)
+            stage_st[base_st + i] = st[j]
+            return c
+
+        lax.fori_loop(0, half, pack, 0)
+        made = send(unit, at, half, (mine, partner))
+        for c in made:
+            c.wait_recv()
+
+        def merge(i, c):
+            j = pick(i, side)
+            ca, cb, both = _merge_stats(st[j], land_st[base_st + i])
+            ca, cb = pltpu.roll(ca, shift, 1), pltpu.roll(cb, shift, 1)
+            for h in range(heads):
+                o = pl.ds(pl.multiple_of(origin + h * HEAD_SIZE, LANE), HEAD_SIZE)
+                acc[i, :, o] = ca[:, h : h + 1] * acc[j, :, o] + cb[:, h : h + 1] * land[
+                    base + i, :, h * HEAD_SIZE : (h + 1) * HEAD_SIZE
+                ].astype(jnp.float32)
+            st[i] = both
+            return c
+
+        lax.fori_loop(0, half, merge, 0)
+        count = half
+        at += half
+        at_st += half
+    final[mine] = acc[0, :, cols].astype(jnp.bfloat16)
+    last = []
+    for d in range(1, grp):
+        c = pltpu.make_async_remote_copy(
+            src_ref=final.at[mine],
+            dst_ref=final.at[mine],
+            send_sem=fsend.at[d - 1],
+            recv_sem=frecv.at[d - 1],
+            device_id=((mine + d) % grp, me),
+            device_id_type=MESH,
+        )
+        c.start()
+        last.append(c)
+    for c in waits:
+        c.wait_send()
+    for c in last:
+        c.wait()
+    for g in range(grp):
+        p = sum(((g >> b) & 1) << (gbits - 1 - b) for b in range(gbits))
+        out_ref[:, p * unit : (p + 1) * unit] = final[g]
 
 
 def on_device(
@@ -209,11 +476,30 @@
     fresh = turn_keys.shape[0]
     base = slots * grp * blk // 2
     size = -(-(slots + fresh) // LANE) * LANE + 2 * BLOCK
-    every_query = lax.all_gather(queries, "blk", axis=0, tiled=True)
-    all_pos = lax.all_gather(turn_pos, "blk", axis=0, tiled=True)
+    rows_in = queries.shape[0]
+    vmem = pl.BlockSpec(memory_space=pltpu.VMEM)
+    moves = blk - 1
+    limit_rows = jnp.broadcast_to((turn_pos - base + 1).astype(jnp.float32)[:, None], (rows_in, LANE))
+    every_query, limits = pl.pallas_call(
+        functools.partial(_gather_kernel, blk, grp),
+        out_shape=(
+            jax.ShapeDtypeStruct((blk, rows_in, queries.shape[1]), jnp.bfloat16),
+            jax.ShapeDtypeStruct((blk, rows_in, LANE), jnp.float32),
+        ),
+        in_specs=[vmem, vmem],
+        out_specs=(vmem, vmem),
+        scratch_shapes=[pltpu.SemaphoreType.DMA]
+        + [pltpu.SemaphoreType.DMA((moves,))] * 4
+        + [pltpu.SemaphoreType.DMA((moves * (grp - 1),))] * 2,
+        compiler_params=pltpu.CompilerParams(
+            collective_id=0, has_side_effects=True, vmem_limit_bytes=24 * 2**20
+        ),
+        name="gather",
+    )(queries, limit_rows)
+    every_query = every_query.reshape(blk * rows_in, queries.shape[1])
+    limits = limits.reshape(blk * rows_in, LANE)
     tokens = every_query.shape[0]
     pad = ((0, LANE - fresh), (0, 0))
-    vmem = pl.BlockSpec(memory_space=pltpu.VMEM)
     smem = pl.BlockSpec(memory_space=pltpu.SMEM)
     kc, vc, code, count = pl.pallas_call(
         functools.partial(_compact_kernel, base, slots, fresh),
@@ -235,17 +521,15 @@
         jnp.pad(turn_values, pad),
     )
     rank = lax.axis_index(("grp", "blk"))
-    limit = (all_pos - base + 1).astype(jnp.float32)
-    index_limit = (jnp.arange(tokens, dtype=jnp.int32) - rank * fresh + 1).astype(jnp.float32)
-    limits = jnp.stack([limit, index_limit], axis=1)
+    first = (rank * fresh).astype(jnp.int32).reshape(1)
     rows = GROUP * tokens
     accum, stats = pl.pallas_call(
         functools.partial(_attend_kernel, fresh),
         out_shape=(
             jax.ShapeDtypeStruct((tokens, QUERY_HEADS * HEAD_SIZE), jnp.float32),
-            jax.ShapeDtypeStruct((tokens, 2 * LANE), jnp.float32),
+            jax.ShapeDtypeStruct((tokens, LANE), jnp.float32),
         ),
-        in_specs=[smem] + [vmem] * 5,
+        in_specs=[smem] * 2 + [vmem] * 5,
         out_specs=(vmem, vmem),
         scratch_shapes=[
             pltpu.VMEM((size // LANE, rows, LANE), jnp.float32),
@@ -254,20 +538,36 @@
         ],
         compiler_params=pltpu.CompilerParams(vmem_limit_bytes=56 * 2**20),
         name="attend",
-    )(count, every_query, kc, vc, code, limits)
-    top, den = stats[:, :QUERY_HEADS], stats[:, LANE : LANE + QUERY_HEADS]
-    highest = lax.pmax(top, ("grp", "blk"))
-    alpha = jnp.exp2(top - highest)
-    scaled = accum.reshape(tokens, QUERY_HEADS, HEAD_SIZE) * alpha[..., None]
-    flat = scaled.reshape(tokens, QUERY_HEADS * HEAD_SIZE)
-    both = jnp.concatenate([flat, den * alpha, jnp.zeros((tokens, LANE - QUERY_HEADS))], axis=1)
-    mine = lax.psum_scatter(both, "blk", scatter_dimension=0, tiled=True)
-    mine = lax.psum(mine, "grp")
-    rows_out = mine.shape[0]
-    num = mine[:, : QUERY_HEADS * HEAD_SIZE].reshape(rows_out, QUERY_HEADS, HEAD_SIZE)
-    dens = mine[:, QUERY_HEADS * HEAD_SIZE : QUERY_HEADS * HEAD_SIZE + QUERY_HEADS]
-    result = num / dens[..., None]
-    return result.reshape(rows_out, QUERY_HEADS * HEAD_SIZE).astype(jnp.bfloat16)
+    )(count, first, every_query, kc, vc, code, limits)
+    unit = QUERY_HEADS * HEAD_SIZE // grp
+    blocks = blk * (grp - 1) + blk - 1
+    stat_blocks = blk * (grp.bit_length() - 1) + blk - 1
+    steps = blk.bit_length() + grp.bit_length() - 2
+    wire = jnp.float32
+    return pl.pallas_call(
+        functools.partial(_reduce_kernel, blk, grp),
+        out_shape=jax.ShapeDtypeStruct((rows_in, QUERY_HEADS * HEAD_SIZE), jnp.bfloat16),
+        in_specs=[vmem] * 2,
+        out_specs=vmem,
+        scratch_shapes=[
+            pltpu.VMEM((blk, rows_in, QUERY_HEADS * HEAD_SIZE), jnp.float32),
+            pltpu.VMEM((blk, rows_in, LANE), jnp.float32),
+            pltpu.VMEM((blocks, rows_in, unit), wire),
+            pltpu.VMEM((stat_blocks, rows_in, LANE), jnp.float32),
+            pltpu.VMEM((blocks, rows_in, unit), wire),
+            pltpu.VMEM((stat_blocks, rows_in, LANE), jnp.float32),
+            pltpu.VMEM((grp, rows_in, unit), jnp.bfloat16),
+        ]
+        + [pltpu.SemaphoreType.DMA((steps,))] * 4
+        + [pltpu.SemaphoreType.DMA((grp - 1,))] * 2,
+        compiler_params=pltpu.CompilerParams(
+            collective_id=1, has_side_effects=True, vmem_limit_bytes=48 * 2**20
+        ),
+        name="reduce",
+    )(
+        accum.reshape(blk, rows_in, QUERY_HEADS * HEAD_SIZE),
+        stats.reshape(blk, rows_in, LANE),
+    )
 
 
 def solution(mesh):

time: 340 us -> 150 us (0.44)
  waiting for transfers between devices: 185 us -> 0 us
  Pallas kernels: 52.7 us -> 132 us
  blocking collectives: 56.6 us -> 0 us
  between operations: 13.9 us -> 0.07 us
  other arithmetic: 8.92 us -> 0.66 us
  local copies, waits for them, and re-layouts: 21.6 us -> 16.9 us
    reduce_scatter x1 -> x0, waiting for transfers between devices: 137 us -> none  [on_device(): mine = lax.psum_scatter(both, 'blk', scatter_dimension=0, tiled=True)]
    pallas_call x0 -> x2, Pallas kernels: none -> 77.1 us  [the longest x1 52.8 us: on_device(): pl.pallas_call(functools.partial(_reduce_kernel, blk, grp), out_shape=jax...]
    pmax x1 -> x0, blocking collectives: 40.4 us -> none  [on_device(): highest = lax.pmax(top, ('grp', 'blk'))]
    all_gather x1 -> x0, waiting for transfers between devices: 27.8 us -> none  [on_device(): every_query = lax.all_gather(queries, 'blk', axis=0, tiled=True)]
    psum x1 -> x0, waiting for transfers between devices: 19.9 us -> none  [on_device(): mine = lax.psum(mine, 'grp')]
    unnamed x1 -> x0, blocking collectives: 16.2 us -> none
    mul x2 -> x0, other arithmetic: 7.12 us -> none  [the longest x1 5.97 us: on_device(): scaled = accum.reshape(tokens, QUERY_HEADS, HEAD_SIZE) * alpha[..., None]]
    concatenate x1 -> x0, local copies, waits for them, and re-layouts: 5.57 us -> none  [on_device(): jnp.concatenate([flat, den * alpha, jnp.zeros((tokens, LANE - QUERY_HEADS...]
  transfers between devices with their start and end apart: 3 -> 0, of which waited for: 3 -> 0; matrix products, arithmetic and copies ran while one was open for 1% -> 0% of each run, Pallas kernels for 2% -> 0%
where the time goes in v2:
time: 150 us; the launch traced here: 149 us
  Pallas kernels  132 us (88%)
  local copies, waits for them, and re-layouts  16.9 us (11%)
    pallas_call x1, Pallas kernels, on_device(): pl.pallas_call(functools.partial(_reduce_kernel, blk, grp), out_shape=jax...  52.8 us
    pallas_call x1, Pallas kernels, on_device(): pl.pallas_call(functools.partial(_attend_kernel, fresh), out_shape=(jax.S...  44.4 us
    pallas_call x1, Pallas kernels, on_device(): pl.pallas_call(functools.partial(_gather_kernel, blk, grp), out_shape=(ja...  24.3 us
    unnamed x23, local copies, waits for them, and re-layouts  15.4 us
    pallas_call x1, Pallas kernels, on_device(): pl.pallas_call(functools.partial(_compact_kernel, base, slots, fresh), ou...  10 us

profile of v2, /device:TPU:0, one launch (start us, length us, event | category | flops | bytes accessed | tf_op | source)
XLA Modules:
  0.0 149.2 jit_solution(2670941917012220960)
XLA Ops:
  0.0 0.7 add_convert_fusion
  0.7 0.1 broadcast_in_dim.2.p_ref
  0.7 0.7 pad.7.tk_ref
  1.5 0.7 pad.8.tv_ref
  2.2 0.0 copy-start.8
  2.2 0.9 copy-done.8
  3.1 24.3 %gather.1 = (bf16[16,16,4096]{2,1,0:T(8,128)(2,1)S(1)}, f32[16,16,128]{2,1,0:T(8,128)S(1)}) custom-call(bf16[16,4096]{1,0:T(8,128)(2,1)S(1)} %copy-done.8, f32[16,128]{1,0:T(8,128)S(1)} %broadcast_in_dim.2.p_ref), custom_call_target="tpu_custom_call" | custom-call | tf_op jit(solution)/shard_map/gather/pallas_call | solution.py:483
  27.4 0.0 copy-start.4
  27.4 1.3 copy-done.4
  28.7 0.0 copy-start.6
  28.7 0.7 copy-done.6
  29.4 0.0 copy-start.1
  29.4 2.2 %copy-done.1 = bf16[2048,1024]{1,0:T(8,128)(2,1)S(1)} copy-done((bf16[2048,1024]{1,0:T(8,128)(2,1)S(1)}, bf16[2048,1024]{1,0:T(8,128)(2,1)}, u32[]{:S(2)}) %copy-start.1) | copy-done | bytes 4194328
  31.6 0.0 copy-start.2
  31.6 2.2 %copy-done.2 = bf16[2048,1024]{1,0:T(8,128)(2,1)S(1)} copy-done((bf16[2048,1024]{1,0:T(8,128)(2,1)S(1)}, bf16[2048,1024]{1,0:T(8,128)(2,1)}, u32[]{:S(2)}) %copy-start.2) | copy-done | bytes 4194328
  33.7 0.0 copy-start.9
  33.7 0.7 copy-done.9
  34.4 10.0 %compact.1 = (bf16[2688,1024]{1,0:T(8,128)(2,1)S(1)}, bf16[2688,1024]{1,0:T(8,128)(2,1)}, f32[16,2688]{1,0:T(8,128)S(1)}, s32[2]{0:T(128)S(1)}) custom-call(s32[16,128]{1,0:T(8,128)S(1)} %bitcast.10, bf16[2048,1024]{1,0:T(8,128)(2,1)S(1)} %copy-done.1, bf16[2048,1024]{1,0:T(8,128)(2,1)S(1)} %copy-done.2, bf16[128,1024]{1,0:T(8,128)(2,1)S(1)} %pad.7.tk_ref, ...), custom_call_target="tpu_custom_call" | custom-call | tf_op jit(solution)/shard_map/compact/pallas_call | solution.py:504
  44.5 0.0 copy-start
  44.5 2.4 %copy-done = bf16[2688,1024]{1,0:T(8,128)(2,1)} copy-done((bf16[2688,1024]{1,0:T(8,128)(2,1)}, bf16[2688,1024]{1,0:T(8,128)(2,1)S(1)}, u32[]{:S(2)}) %copy-start) | copy-done | bytes 5505048
  46.9 0.0 copy-start.5
  46.9 0.7 copy-done.5
  47.6 0.0 copy-start.10
  47.6 0.6 copy-done.10
  48.2 44.4 %attend.1 = (f32[256,4096]{1,0:T(8,128)}, f32[256,128]{1,0:T(8,128)}) custom-call(s32[2]{0:T(128)} %copy-done.10, s32[1]{0:T(128)} %bitcast.1.first_ref, bf16[256,4096]{1,0:T(8,128)(2,1)} %bitcast.7, bf16[2688,1024]{1,0:T(8,128)(2,1)} %copy-done, bf16[2688,1024]{1,0:T(8,128)(2,1)} %get-tuple-element.16.vc_ref, f32[16,2688]{1,0:T(8,128)} %copy-done.5, ...), custom_call_target="tpu_custom_call" | custom-call | tf_op jit(solution)/shard_map/attend/pallas_call | solution.py:526
  92.6 0.0 copy-start.3
  92.6 2.2 %copy-done.3 = f32[256,4096]{1,0:T(8,128)S(1)} copy-done((f32[256,4096]{1,0:T(8,128)S(1)}, f32[256,4096]{1,0:T(8,128)}, u32[]{:S(2)}) %copy-start.3) | copy-done | bytes 4194328
  94.7 0.0 copy-start.7
  94.7 0.9 copy-done.7
  95.6 52.8 %reduce.1 = bf16[16,4096]{1,0:T(8,128)(2,1)S(1)} custom-call(f32[16,16,4096]{2,1,0:T(8,128)S(1)} %bitcast.6, f32[16,16,128]{2,1,0:T(8,128)S(1)} %bitcast.9), custom_call_target="tpu_custom_call" | custom-call | tf_op jit(solution)/shard_map/reduce/pallas_call | solution.py:547
  148.5 0.7 copy.9
Async XLA Ops:
  2.2 0.9 copy-start.8
  27.4 1.3 copy-start.4
  28.7 0.7 copy-start.6
  29.4 2.2 %copy-start.1 = (bf16[2048,1024]{1,0:T(8,128)(2,1)S(1)}, bf16[2048,1024]{1,0:T(8,128)(2,1)}, u32[]{:S(2)}) copy-start(bf16[2048,1024]{1,0:T(8,128)(2,1)} %k_ref.1) | copy-start | bytes 12582916
  31.6 2.2 %copy-start.2 = (bf16[2048,1024]{1,0:T(8,128)(2,1)S(1)}, bf16[2048,1024]{1,0:T(8,128)(2,1)}, u32[]{:S(2)}) copy-start(bf16[2048,1024]{1,0:T(8,128)(2,1)} %v_ref.1) | copy-start | bytes 12582916
  33.7 0.7 copy-start.9
  44.5 2.5 %copy-start = (bf16[2688,1024]{1,0:T(8,128)(2,1)}, bf16[2688,1024]{1,0:T(8,128)(2,1)S(1)}, u32[]{:S(2)}) copy-start(bf16[2688,1024]{1,0:T(8,128)(2,1)S(1)} %get-tuple-element.15.kc_ref) | copy-start | bytes 16515076
  46.9 0.7 copy-start.5
  47.6 0.6 copy-start.10
  92.6 2.2 %copy-start.3 = (f32[256,4096]{1,0:T(8,128)S(1)}, f32[256,4096]{1,0:T(8,128)}, u32[]{:S(2)}) copy-start(f32[256,4096]{1,0:T(8,128)} %get-tuple-element.19) | copy-start | bytes 12582916
  94.7 0.9 copy-start.7
